TPU v7x, 32 devices: a whole 2x2x4 slice. The times are simulated.
32 devices in a mesh: parts: 2 (over y), shard: 2 (over core), blk: 8 (over z, x).
Axes of the slice: x: 2, y: 2, z: 4, core: 2. Of those that a mesh axis runs over, the one named last changes fastest.
Arguments:
- queries_in: bfloat16 [4096, 1024], P(('parts', 'shard', 'blk')), parts along dimension 0, may hold values from -12 to 12
- query_weight: bfloat16 [1024, 1024], replicated, may hold values from -0.1875 to 0.1875
- bank: bfloat16 [2048, 1024], P(('parts', 'shard', 'blk')), parts along dimension 0, may hold values from -110 to 110
- uses: int32 [4096, 2], P(('parts', 'shard', 'blk')), parts along dimension 0, may hold values from 0 to 1, as said below
Outputs:
- retrieved: bfloat16 [4096, 1024], P(('parts', 'shard', 'blk')), parts along dimension 0
There are 2 independent parts, one for each index of `parts`. A program takes and returns all parts, laid end to end along the dimension named above; an argument that names none is the same for every part. Nothing has to cross between parts.
Inputs may be any that keep to these rules, and one draw needn't show every extreme that they name: `uses`: every query lists one or both of the two shards. Of the 128 queries of one device, at most 128 list one shard, and in every draw for every index of blk the queries of both devices at that index all list one same shard.
All inputs are finite; a program needn't handle non-finite values.
Results may differ from a plain program's by a relative error of at most 0.035.
Values may be sent and summed in bfloat16 or wider, within the bound.
A program may use at most 128 MiB of HBM per device.

v0:
```python
import math
import jax
import jax.numpy as jnp
from jax import lax
from jax.sharding import PartitionSpec as P

HEADS = 8
HEAD_DIM = 128
NEGATIVE = -1e30


def empty_carry(slot_count):
    return (
        jnp.full((slot_count, HEADS), NEGATIVE, jnp.float32),
        jnp.zeros((slot_count, HEADS), jnp.float32),
        jnp.zeros((slot_count, HEADS, HEAD_DIM), jnp.float32),
    )


def fold_piece(carry, query_heads, piece, allowed):
    slot_count = query_heads.shape[0]
    piece_rows = piece.shape[0]
    key_rows = math.gcd(piece_rows, 512)
    key_blocks = piece_rows // key_rows
    keys_blocked = piece.reshape(key_blocks, key_rows, HEADS, HEAD_DIM)
    mask_blocked = allowed.reshape(slot_count, key_blocks, key_rows).transpose(1, 0, 2)
    block_rows = math.gcd(slot_count, 128)
    blocks = slot_count // block_rows
    logit_scale = HEAD_DIM ** (-0.5)

    def blocked(array):
        return array.reshape((blocks, block_rows) + array.shape[1:])

    def key_step(state, inputs):
        keys_piece, mask_all = inputs

        def one_block(block_inputs):
            query_block, mask_block, top_old, total_old, accum_old = block_inputs
            scores = (
                jnp.einsum(
                    "shd,rhd->shr", query_block, keys_piece, preferred_element_type=jnp.float32
                )
                * logit_scale
            )
            scores = jnp.where(mask_block[:, None, :], scores, NEGATIVE)
            top_new = jnp.maximum(top_old, jnp.max(scores, axis=-1))
            weights = jnp.where(mask_block[:, None, :], jnp.exp(scores - top_new[..., None]), 0.0)
            factor = jnp.exp(top_old - top_new)
            total_new = total_old * factor + jnp.sum(weights, axis=-1)
            accum_new = accum_old * factor[..., None] + jnp.einsum(
                "shr,rhd->shd",
                weights.astype(jnp.bfloat16),
                keys_piece,
                preferred_element_type=jnp.float32,
            )
            return (top_new, total_new, accum_new)

        top_old, total_old, accum_old = state
        results = lax.map(
            one_block,
            (
                blocked(query_heads),
                blocked(mask_all),
                blocked(top_old),
                blocked(total_old),
                blocked(accum_old),
            ),
        )
        return (
            tuple((result.reshape((slot_count,) + result.shape[2:]) for result in results)),
            None,
        )

    final, unused = lax.scan(key_step, carry, (keys_blocked, mask_blocked))
    return final


def local(queries_in, query_weight, bank, uses):
    row_count = queries_in.shape[0]
    width_all = HEADS * HEAD_DIM
    projected = jnp.dot(queries_in, query_weight, preferred_element_type=jnp.float32).astype(
        jnp.bfloat16
    )
    positions = jnp.cumsum(uses, axis=0) - 1
    listed = uses > 0
    onehot_table = (positions.T[:, None, :] == jnp.arange(row_count)[None, :, None]) & listed.T[
        :, None, :
    ]
    outgoing = jnp.einsum(
        "sct,td->scd",
        onehot_table.astype(jnp.bfloat16),
        projected,
        preferred_element_type=jnp.float32,
    ).astype(jnp.bfloat16)
    incoming = lax.all_to_all(outgoing, "shard", split_axis=0, concat_axis=0, tiled=True)
    item_count = incoming.shape[1]
    slot_heads = incoming.reshape(2 * item_count, HEADS, HEAD_DIM)
    piece = lax.all_gather(bank, "blk", axis=0, tiled=True)
    allowed = jnp.ones((2 * item_count, piece.shape[0]), dtype=jnp.bool_)
    top_part, total_part, accum_part = fold_piece(
        empty_carry(2 * item_count), slot_heads, piece, allowed
    )
    accum_back = lax.all_to_all(
        accum_part.reshape(2, item_count, width_all).astype(jnp.bfloat16),
        "shard",
        split_axis=0,
        concat_axis=0,
        tiled=True,
    ).astype(jnp.float32)
    top_back = lax.all_to_all(
        top_part.reshape(2, item_count, HEADS).astype(jnp.bfloat16),
        "shard",
        split_axis=0,
        concat_axis=0,
        tiled=True,
    ).astype(jnp.float32)
    total_back = lax.all_to_all(
        total_part.reshape(2, item_count, HEADS).astype(jnp.bfloat16),
        "shard",
        split_axis=0,
        concat_axis=0,
        tiled=True,
    ).astype(jnp.float32)
    safe_slot = jnp.clip(positions, 0, row_count - 1)
    top_pair = jnp.stack(
        [jnp.take(top_back[member], safe_slot[:, member], axis=0) for member in range(2)], 1
    )
    total_pair = jnp.stack(
        [jnp.take(total_back[member], safe_slot[:, member], axis=0) for member in range(2)], 1
    )
    accum_pair = jnp.stack(
        [jnp.take(accum_back[member], safe_slot[:, member], axis=0) for member in range(2)], 1
    )
    accum_pair = accum_pair.reshape(row_count, 2, HEADS, HEAD_DIM)
    top_pair = jnp.where(listed[:, :, None], top_pair, NEGATIVE)
    highest = jnp.max(top_pair, axis=1)
    scale_pair = jnp.where(listed[:, :, None], jnp.exp(top_pair - highest[:, None, :]), 0.0)
    total_all = jnp.sum(scale_pair * total_pair, axis=1)
    accum_all = jnp.sum(scale_pair[..., None] * accum_pair, axis=1)
    return (accum_all / total_all[..., None]).reshape(row_count, width_all).astype(jnp.bfloat16)


def solution(mesh):
    in_specs = (
        P(("parts", "shard", "blk"), None),
        P(),
        P(("parts", "shard", "blk"), None),
        P(("parts", "shard", "blk"), None),
    )
    out_specs = P(("parts", "shard", "blk"), None)
    return jax.shard_map(local, mesh=mesh, in_specs=in_specs, out_specs=out_specs, check_vma=False)
```

profile of v0, /device:TPU:1, one launch (start us, length us, event | category | flops | bytes accessed | tf_op | source)
XLA Modules:
  0.0 94.7 jit_solution(11347580435513448345)
XLA Ops:
  6.5 0.7 all-gather.2.cloned.1.call-update
  7.3 0.8 copy.41
  8.1 0.2 reduce_window_sum.11
  8.4 2.4 %convolution_convert_fusion = bf16[2,128,1024]{2,1,0:T(8,128)(2,1)} fusion(bf16[128,1024]{1,0:T(8,128)(2,1)} %param.10, bf16[1024,1024]{1,0:T(8,128)(2,1)S(1)} %copy-done, s32[2,128]{1,0:T(2,128)S(1)} %copy.44, pred[2,128]{1,0:T(4,128)(4,1)S(1)} %copy.45), kind=kOutput, calls=%fused_computation.29 | convolution fusion | flops 336003072 | bytes 2884864 | tf_op jit(solution)/shard_map/sct,td->scd/dot_general | solution.py:89
  10.8 3.5 %all-to-all-start = ((bf16[2,128,1024]{2,1,0:T(8,128)(2,1)}), bf16[2,128,1024]{2,1,0:T(8,128)(2,1)S(1)}, u32[]{:S(2)}, u32[]{:S(2)}) async-start(bf16[2,128,1024]{2,1,0:T(8,128)(2,1)} %convolution_convert_fusion), calls=%async_computation | async-start | bytes 1048576 | tf_op jit(solution)/shard_map/all_to_all | solution.py:95
  14.5 1.3 %all-to-all-done = bf16[2,128,1024]{2,1,0:T(8,128)(2,1)S(1)} async-done(((bf16[2,128,1024]{2,1,0:T(8,128)(2,1)}), bf16[2,128,1024]{2,1,0:T(8,128)(2,1)S(1)}, u32[]{:S(2)}, u32[]{:S(2)}) %all-to-all-start) | async-done | bytes 524320 | tf_op jit(solution)/shard_map/all_to_all | solution.py:95
  15.7 0.9 copy.60
  16.6 0.2 slice_reduce_fusion.1
  16.9 33.9 %all-gather.2.cloned.1.call-done = bf16[512,1024]{1,0:T(8,128)(2,1)} async-done(((bf16[64,1024]{1,0:T(8,128)(2,1)}), bf16[512,1024]{1,0:T(8,128)(2,1)}) %all-gather.2.cloned.1.call-update) | async-done | bytes 1048592 | tf_op jit(solution)/shard_map/all_gather | solution.py:98
  50.8 2.3 %copy.46 = bf16[512,1024]{0,1:T(8,128)(2,1)} copy(bf16[512,1024]{1,0:T(8,128)(2,1)} %all-gather.2.cloned.1.call-done) | data formatting | bytes 2097152 | tf_op jit(solution)/shard_map/all_gather | solution.py:98
  53.1 1.6 %copy.48 = bf16[512,8,128]{2,0,1:T(8,128)(2,1)S(1)} copy(bf16[512,8,128]{0,2,1:T(8,128)(2,1)} %bitcast.121) | data formatting | bytes 2097152 | tf_op jit(solution)/shard_map/while/body/eval_jaxpr/while | solution.py:59
  54.7 7.4 %while.26 = (s32[]{:T(128)}, bf16[2,128,8]{1,2,0:T(8,128)(2,1)S(1)}, bf16[2,128,8]{1,2,0:T(8,128)(2,1)}, bf16[2,128,8,128]{3,1,2,0:T(8,128)(2,1)}, bf16[2,128,8,...) while((s32[]{:T(128)}, bf16[2,128,8]{1,2,0:T(8,128)(2,1)S(1)}, ...), condition=%wide.region_4.5_spmd, body=%wide.region_1.4_spmd.sunk | while | flops 272768000 | bytes 13944989 | solution.py:59
  54.7 1.0 %constant_dynamic-slice_fusion.2 = bf16[1,128,8,128]{3,2,1,0:T(8,128)(2,1)S(1)} fusion(bf16[2,128,8,128]{3,2,1,0:T(8,128)(2,1)} %get-tuple-element.220, s32[]{:T(128)S(6)} %copy.80), kind=kLoop, calls=%fused_computation.27.clone.1 | loop fusion | bytes 524292 | tf_op jit(solution)/shard_map/while/body/eval_jaxpr/while/body/jit(dynamic_index_in_dim)/dynamic_slice | solution.py:59
  55.7 0.5 bitcast_reduce_fusion.2
  56.2 0.6 fusion.37
  56.8 0.7 fusion.39
  57.6 0.7 fusion.38
  58.2 0.1 copy-done.3
  58.4 1.0 %constant_dynamic-slice_fusion.2 = bf16[1,128,8,128]{3,2,1,0:T(8,128)(2,1)S(1)} fusion(bf16[2,128,8,128]{3,2,1,0:T(8,128)(2,1)} %get-tuple-element.220, s32[]{:T(128)S(6)} %copy.80), kind=kLoop, calls=%fused_computation.27.clone.1 | loop fusion | bytes 524292 | tf_op jit(solution)/shard_map/while/body/eval_jaxpr/while/body/jit(dynamic_index_in_dim)/dynamic_slice | solution.py:59
  59.4 0.5 bitcast_reduce_fusion.2
  59.9 0.6 fusion.37
  60.5 0.7 fusion.39
  61.3 0.7 fusion.38
  61.9 0.1 copy-done.3
  62.1 1.9 %copy_bitcast_fusion.2 = bf16[2,128,1024]{2,1,0:T(8,128)(2,1)} fusion(bf16[2,128,8,128]{3,1,2,0:T(8,128)(2,1)} %get-tuple-element.95), kind=kLoop, calls=%fused_computation.34 | loop fusion | bytes 1048576 | tf_op jit(solution)/shard_map/convert_element_type | solution.py:104
  64.0 5.0 %all_to_all.20 = bf16[2,128,8]{1,2,0:T(8,128)(2,1)S(1)} all-to-all(bf16[2,128,8]{1,2,0:T(8,128)(2,1)S(1)} %get-tuple-element.94), channel_id=1, replica_groups=mesh['parts'=2,'shard'=2,'blk'=8] {'shard'}, dimensions={0} | all-to-all | bytes 8192 | tf_op jit(solution)/shard_map/all_to_all | solution.py:110
  69.0 3.5 %all-to-all-start.3 = ((bf16[2,128,8]{1,2,0:T(8,128)(2,1)}), bf16[2,128,8]{1,2,0:T(8,128)(2,1)S(1)}, u32[]{:S(2)}, u32[]{:S(2)}) async-start(bf16[2,128,8]{1,2,0:T(8,128)(2,1)} %get-tuple-element.96), calls=%async_computation.3 | async-start | bytes 8192 | tf_op jit(solution)/shard_map/all_to_all | solution.py:117
  72.5 0.1 copy.49
  72.7 0.9 all-to-all-done.3
  73.6 3.8 %all-to-all-start.2 = ((bf16[2,128,1024]{2,1,0:T(8,128)(2,1)}), bf16[2,128,1024]{2,1,0:T(8,128)(2,1)S(1)}, u32[]{:S(2)}, u32[]{:S(2)}) async-start(bf16[2,128,1024]{2,1,0:T(8,128)(2,1)} %copy_bitcast_fusion.2), calls=%async_computation.2 | async-start | bytes 1048576 | tf_op jit(solution)/shard_map/all_to_all | solution.py:103
  77.4 0.1 copy.54
  77.5 0.6 gather_fusion
  78.2 0.6 gather_fusion.4
  79.0 0.7 gather_fusion.1
  79.7 0.6 gather_fusion.5
  80.6 0.1 copy.57
  80.7 0.1 copy.52
  80.9 0.1 convert_element_type.45
  81.0 1.6 %gather_fusion.2 = f32[128,1024]{1,0:T(8,128)} fusion(f32[128,1024]{1,0:T(8,128)S(1)} %get-tuple-element.141, s32[1024]{0:T(1024)S(1)} %pad_clamp_fusion.1), kind=kCustom, calls=%fused_computation.1.clone | custom fusion | bytes 1049088 | tf_op jit(solution)/shard_map/jit(_take)/gather | solution.py:132
  82.6 1.1 %select_bitcast_fusion.1 = f32[16,8,8,128]{3,1,2,0:T(8,128)S(1)} fusion(f32[128,1024]{1,0:T(8,128)} %gather_fusion.2, pred[128]{0:T(512)(128)(4,1)S(1)} %get-tuple-element.156), kind=kLoop, calls=%fused_computation.38 | loop fusion | flops 131072 | bytes 1048704
  83.8 0.9 copy.61
  84.7 0.8 gather_fusion.3
  85.5 0.1 select_bitcast_fusion
  85.6 0.1 copy.62
  85.7 0.8 copy-done.1
  86.5 0.3 fusion.15
  86.8 0.2 divide_convert_fusion
  87.1 0.8 copy.70
  (41 shorter events, 0.9 us)
Async XLA Ops:
  6.5 1.9 %copy-start = (bf16[1024,1024]{1,0:T(8,128)(2,1)S(1)}, bf16[1024,1024]{1,0:T(8,128)(2,1)}, u32[]{:S(2)}) copy-start(bf16[1024,1024]{1,0:T(8,128)(2,1)} %param.11) | copy-start | bytes 6291460
  6.5 44.3 %all-gather.2.cloned.1.call-start = ((), (), s32[]{:S(2)}) async-start(), calls=%async_computation.4 | async-start | bytes 1179648 | tf_op jit(solution)/shard_map/all_gather | solution.py:98
  10.8 4.9 %all-to-all-start = ((bf16[2,128,1024]{2,1,0:T(8,128)(2,1)}), bf16[2,128,1024]{2,1,0:T(8,128)(2,1)S(1)}, u32[]{:S(2)}, u32[]{:S(2)}) async-start(bf16[2,128,1024]{2,1,0:T(8,128)(2,1)} %convolution_convert_fusion), calls=%async_computation | async-start | bytes 1048576 | tf_op jit(solution)/shard_map/all_to_all | solution.py:95
  55.7 1.1 %copy-start.2 = (bf16[2,128,8,128]{3,1,2,0:T(8,128)(2,1)S(1)}, bf16[2,128,8,128]{3,1,2,0:T(8,128)(2,1)}, u32[]{:S(2)}) copy-start(bf16[2,128,8,128]{3,1,2,0:T(8,128)(2,1)} %get-tuple-element.212) | copy-start | bytes 1572868 | tf_op jit(solution)/shard_map/while/body/eval_jaxpr/while
  57.6 0.8 copy-start.3
  59.4 1.1 %copy-start.2 = (bf16[2,128,8,128]{3,1,2,0:T(8,128)(2,1)S(1)}, bf16[2,128,8,128]{3,1,2,0:T(8,128)(2,1)}, u32[]{:S(2)}) copy-start(bf16[2,128,8,128]{3,1,2,0:T(8,128)(2,1)} %get-tuple-element.212) | copy-start | bytes 1572868 | tf_op jit(solution)/shard_map/while/body/eval_jaxpr/while
  61.3 0.8 copy-start.3
  69.0 4.6 %all-to-all-start.3 = ((bf16[2,128,8]{1,2,0:T(8,128)(2,1)}), bf16[2,128,8]{1,2,0:T(8,128)(2,1)S(1)}, u32[]{:S(2)}, u32[]{:S(2)}) async-start(bf16[2,128,8]{1,2,0:T(8,128)(2,1)} %get-tuple-element.96), calls=%async_computation.3 | async-start | bytes 8192 | tf_op jit(solution)/shard_map/all_to_all | solution.py:117
  73.6 7.3 %all-to-all-start.2 = ((bf16[2,128,1024]{2,1,0:T(8,128)(2,1)}), bf16[2,128,1024]{2,1,0:T(8,128)(2,1)S(1)}, u32[]{:S(2)}, u32[]{:S(2)}) async-start(bf16[2,128,1024]{2,1,0:T(8,128)(2,1)} %copy_bitcast_fusion.2), calls=%async_computation.2 | async-start | bytes 1048576 | tf_op jit(solution)/shard_map/all_to_all | solution.py:103
  85.5 1.0 %copy-start.1 = (f32[16,8,8,128]{3,2,1,0:T(8,128)S(1)}, f32[16,8,8,128]{3,2,1,0:T(8,128)}, u32[]{:S(2)}) copy-start(f32[16,8,8,128]{3,2,1,0:T(8,128)} %copy.61) | copy-start | bytes 1572868
Sparse Core Ops, SparseCore 0:
  9.5 41.2 all-gather.1
where the time goes:
time: 95.3 us; the launch traced here: 94.7 us
  waiting for transfers between devices  36.8 us (39%)
  local copies, waits for them, and re-layouts  18.4 us (19%)
  between operations  13.6 us (14%)
  starting transfers between devices  10.9 us (11%)
  blocking collectives  5.01 us (5%)
  matrix products  4.94 us (5%)
  other arithmetic  4.87 us (5%)
    all_gather x1, waiting for transfers between devices, local(): piece = lax.all_gather(bank, 'blk', axis=0, tiled=True)  33.9 us
    all_to_all x1, blocking collectives, local(): lax.all_to_all(top_part.reshape(2, item_count, HEADS).astype(jnp.bfloat16...  5.01 us
    unnamed x9, local copies, waits for them, and re-layouts  4.23 us
    all_to_all x1, starting transfers between devices, local(): lax.all_to_all(accum_part.reshape(2, item_count, width_all).astype(jnp.bf...  3.81 us
    all_to_all x1, starting transfers between devices, local(): lax.all_to_all(total_part.reshape(2, item_count, HEADS).astype(jnp.bfloat...  3.55 us
    all_to_all x1, starting transfers between devices, local(): lax.all_to_all(outgoing, 'shard', split_axis=0, concat_axis=0, tiled=True)  3.53 us
    dot_general x1, matrix products, local(): jnp.einsum('sct,td->scd', onehot_table.astype(jnp.bfloat16), projected, p...  2.43 us
    gather x2, local copies, waits for them, and re-layouts, local(): jnp.take(accum_back[member], safe_slot[:, member], axis=0)  2.38 us
  transfers between devices with their start and end apart: 4, of which 3 were waited for; matrix products, arithmetic and copies ran while one was open for 9% of the time, Pallas kernels for 0%

commit v1 on v0

--- a/solution.py
+++ b/solution.py
@@ -95,7 +95,12 @@
     incoming = lax.all_to_all(outgoing, "shard", split_axis=0, concat_axis=0, tiled=True)
     item_count = incoming.shape[1]
     slot_heads = incoming.reshape(2 * item_count, HEADS, HEAD_DIM)
-    piece = lax.all_gather(bank, "blk", axis=0, tiled=True)
+    ring = [bank]
+    for hop in range(7):
+        ring.append(lax.ppermute(ring[-1], "blk", [(dev, (dev + 1) % 8) for dev in range(8)]))
+    piece = jnp.roll(
+        jnp.concatenate(ring[::-1], axis=0), (lax.axis_index("blk") + 1) * ring[0].shape[0], axis=0
+    )
     allowed = jnp.ones((2 * item_count, piece.shape[0]), dtype=jnp.bool_)
     top_part, total_part, accum_part = fold_piece(
         empty_carry(2 * item_count), slot_heads, piece, allowed

time: 95.3 us -> 115 us (1.21)
  between operations: 13.6 us -> 0.24 us
  waiting for transfers between devices: 36.8 us -> 49.9 us
  local copies, waits for them, and re-layouts: 18.4 us -> 27.6 us
  blocking collectives: 5.01 us -> 10.9 us
  starting transfers between devices: 10.9 us -> 15.1 us
    ppermute x0 -> x7, waiting for transfers between devices: none -> 49 us  [local(): lax.ppermute(ring[-1], 'blk', [(dev, (dev + 1) % 8) for dev in range(8)])]
    all_gather x1 -> x0, waiting for transfers between devices: 33.9 us -> none  [local(): piece = lax.all_gather(bank, 'blk', axis=0, tiled=True)]
    concatenate x0 -> x1, local copies, waits for them, and re-layouts: none -> 5.97 us  [local(): jnp.roll(jnp.concatenate(ring[::-1], axis=0), (lax.axis_index('blk') + 1)...]
    all_to_all x1, blocking collectives: 5.01 us -> 10.9 us  [local(): lax.all_to_all(top_part.reshape(2, item_count, HEADS).astype(jnp.bfloat16...]
    dynamic_slice x0 -> x1, local copies, waits for them, and re-layouts: none -> 2.77 us  [local(): jnp.roll(jnp.concatenate(ring[::-1], axis=0), (lax.axis_index('blk') + 1)...]
    unnamed x9 -> x14, local copies, waits for them, and re-layouts: 4.23 us -> 6.91 us
    all_gather x1 -> x0, local copies, waits for them, and re-layouts: 2.28 us -> none  [local(): piece = lax.all_gather(bank, 'blk', axis=0, tiled=True)]
    ppermute x0 -> x7, starting transfers between devices: none -> 2.11 us  [local(): lax.ppermute(ring[-1], 'blk', [(dev, (dev + 1) % 8) for dev in range(8)])]
  transfers between devices with their start and end apart: 4 -> 10, of which waited for: 3 -> 8; matrix products, arithmetic and copies ran while one was open for 9% -> 7% of each run, Pallas kernels for 0% -> 0%
where the time goes in v1:
time: 115 us; the launch traced here: 114 us
  waiting for transfers between devices  49.9 us (43%)
  local copies, waits for them, and re-layouts  27.6 us (24%)
  starting transfers between devices  15.1 us (13%)
  blocking collectives  10.9 us (9%)
  matrix products  4.98 us (4%)
  other arithmetic  4.85 us (4%)
    ppermute x7, waiting for transfers between devices, local(): lax.ppermute(ring[-1], 'blk', [(dev, (dev + 1) % 8) for dev in range(8)])  49 us
    all_to_all x1, blocking collectives, local(): lax.all_to_all(top_part.reshape(2, item_count, HEADS).astype(jnp.bfloat16...  10.9 us
    unnamed x14, local copies, waits for them, and re-layouts  6.91 us
    concatenate x1, local copies, waits for them, and re-layouts, local(): jnp.roll(jnp.concatenate(ring[::-1], axis=0), (lax.axis_index('blk') + 1)...  5.97 us
    all_to_all x1, starting transfers between devices, local(): lax.all_to_all(outgoing, 'shard', split_axis=0, concat_axis=0, tiled=True)  5.62 us
    all_to_all x1, starting transfers between devices, local(): lax.all_to_all(accum_part.reshape(2, item_count, width_all).astype(jnp.bf...  3.81 us
    all_to_all x1, starting transfers between devices, local(): lax.all_to_all(total_part.reshape(2, item_count, HEADS).astype(jnp.bfloat...  3.52 us
    dynamic_slice x1, local copies, waits for them, and re-layouts, local(): jnp.roll(jnp.concatenate(ring[::-1], axis=0), (lax.axis_index('blk') + 1)...  2.77 us
  transfers between devices with their start and end apart: 10, of which 8 were waited for; matrix products, arithmetic and copies ran while one was open for 7% of the time, Pallas kernels for 0%

profile of v1, /device:TPU:1, one launch (start us, length us, event | category | flops | bytes accessed | tf_op | source)
XLA Modules:
  0.0 113.7 jit_solution(7580701990203605243)
XLA Ops:
  0.0 1.2 %copy.50 = bf16[64,1024]{0,1:T(8,128)(2,1)S(1)} copy(bf16[64,1024]{1,0:T(8,128)(2,1)} %param.12) | data formatting | bytes 262144 | tf_op args[2]
  1.2 2.1 %collective-permute-start = (bf16[64,1024]{0,1:T(8,128)(2,1)S(1)}, bf16[64,1024]{0,1:T(8,128)(2,1)S(1)}, u32[]{:S(2)}, u32[]{:S(2)}) collective-permute-start(bf16[64,1024]{0,1:T(8,128)(2,1)S(1)} %copy.50), channel_id=1, source_target_pairs={{0,1},{1,2},{2,3},{3,4},{4,5},{5,6},{6,7},{7,0},{8,9},{9,10},{10,1... | collective-permute-start | bytes 393224 | tf_op jit(solution)/shard_map/ppermute | solution.py:100
  3.3 0.8 copy.45
  4.2 0.2 reduce_window_sum.11
  4.4 8.0 %collective-permute-done = bf16[64,1024]{0,1:T(8,128)(2,1)S(1)} collective-permute-done((bf16[64,1024]{0,1:T(8,128)(2,1)S(1)}, bf16[64,1024]{0,1:T(8,128)(2,1)S(1)}, u32[]{:S(2)}, u32[]{:S(2)}) %collective-permute-start) | collective-permute-done | bytes 131104 | tf_op jit(solution)/shard_map/ppermute | solution.py:100
  12.5 9.2 %collective-permute-done.1 = bf16[64,1024]{0,1:T(8,128)(2,1)S(1)} collective-permute-done((bf16[64,1024]{0,1:T(8,128)(2,1)S(1)}, bf16[64,1024]{0,1:T(8,128)(2,1)S(1)}, u32[]{:S(2)}, u32[]{:S(2)}) %collective-permute-start.1) | collective-permute-done | bytes 131104 | tf_op jit(solution)/shard_map/ppermute | solution.py:100
  21.7 2.4 %convolution_convert_fusion = bf16[2,128,1024]{2,1,0:T(8,128)(2,1)} fusion(bf16[128,1024]{1,0:T(8,128)(2,1)} %param.10, bf16[1024,1024]{1,0:T(8,128)(2,1)S(1)} %copy-done, s32[2,128]{1,0:T(2,128)S(1)} %copy.48, pred[2,128]{1,0:T(4,128)(4,1)S(1)} %copy.49), kind=kOutput, calls=%fused_computation.29 | convolution fusion | flops 336003072 | bytes 2884864 | tf_op jit(solution)/shard_map/sct,td->scd/dot_general | solution.py:89
  24.1 5.6 %all-to-all-start = ((bf16[2,128,1024]{2,1,0:T(8,128)(2,1)}), bf16[2,128,1024]{2,1,0:T(8,128)(2,1)S(1)}, u32[]{:S(2)}, u32[]{:S(2)}) async-start(bf16[2,128,1024]{2,1,0:T(8,128)(2,1)} %convolution_convert_fusion), calls=%async_computation | async-start | bytes 1048576 | tf_op jit(solution)/shard_map/all_to_all | solution.py:95
  29.7 0.4 collective-permute-done.2
  30.1 0.2 slice_reduce_fusion.1
  30.3 7.9 %collective-permute-done.3 = bf16[64,1024]{0,1:T(8,128)(2,1)S(1)} collective-permute-done((bf16[64,1024]{0,1:T(8,128)(2,1)}, bf16[64,1024]{0,1:T(8,128)(2,1)S(1)}, u32[]{:S(2)}, u32[]{:S(2)}) %collective-permute-start.3) | collective-permute-done | bytes 131104 | tf_op jit(solution)/shard_map/ppermute | solution.py:100
  38.2 0.7 copy-done.2
  39.0 7.9 %collective-permute-done.4 = bf16[64,1024]{0,1:T(8,128)(2,1)S(1)} collective-permute-done((bf16[64,1024]{0,1:T(8,128)(2,1)S(1)}, bf16[64,1024]{0,1:T(8,128)(2,1)S(1)}, u32[]{:S(2)}, u32[]{:S(2)}) %collective-permute-start.4) | collective-permute-done | bytes 131104 | tf_op jit(solution)/shard_map/ppermute | solution.py:100
  46.9 0.7 copy-done.3
  47.6 8.0 %collective-permute-done.5 = bf16[64,1024]{0,1:T(8,128)(2,1)} collective-permute-done((bf16[64,1024]{0,1:T(8,128)(2,1)S(1)}, bf16[64,1024]{0,1:T(8,128)(2,1)}, u32[]{:S(2)}, u32[]{:S(2)}) %collective-permute-start.5) | collective-permute-done | bytes 131104 | tf_op jit(solution)/shard_map/ppermute | solution.py:100
  55.8 0.9 copy.66
  56.7 7.6 %collective-permute-done.6 = bf16[64,1024]{0,1:T(8,128)(2,1)} collective-permute-done((bf16[64,1024]{0,1:T(8,128)(2,1)}, bf16[64,1024]{0,1:T(8,128)(2,1)}, u32[]{:S(2)}, u32[]{:S(2)}) %collective-permute-start.6) | collective-permute-done | bytes 131104 | tf_op jit(solution)/shard_map/ppermute | solution.py:100
  64.2 6.0 %concatenate.11 = bf16[1024,1024]{0,1:T(8,128)(2,1)} concatenate(bf16[64,1024]{0,1:T(8,128)(2,1)} %collective-permute-done.6, bf16[64,1024]{0,1:T(8,128)(2,1)} %collective-permute-done.5, bf16[64,1024]{0,1:T(8,128)(2,1)} %copy-done.3, bf16[64,1024]{0,1:T(8,128)(2,1)} %copy-done.2, bf16[64,1024]{0,1:T(8,128)(2,1)} %collective-permute-done.2, ...), dimensions={0} | concatenate | bytes 4194304 | tf_op jit(solution)/shard_map/jit(_roll_dynamic)/concatenate | solution.py:101
  70.2 2.8 %constant_dynamic-slice_fusion.1 = bf16[512,1024]{0,1:T(8,128)(2,1)} fusion(bf16[1024,1024]{0,1:T(8,128)(2,1)} %concatenate.11, s32[]{:T(128)S(6)} %select_n.49), kind=kLoop, calls=%fused_computation.70 | loop fusion | bytes 2097156 | tf_op jit(solution)/shard_map/jit(_roll_dynamic)/dynamic_slice | solution.py:101
  73.0 1.6 %copy.54 = bf16[512,8,128]{2,0,1:T(8,128)(2,1)S(1)} copy(bf16[512,8,128]{0,2,1:T(8,128)(2,1)} %bitcast.121) | data formatting | bytes 2097152 | tf_op jit(solution)/shard_map/while/body/eval_jaxpr/while | solution.py:59
  74.6 7.4 %while.26 = (s32[]{:T(128)}, bf16[2,128,8]{1,2,0:T(8,128)(2,1)S(1)}, bf16[2,128,8]{1,2,0:T(8,128)(2,1)}, bf16[2,128,8,128]{3,1,2,0:T(8,128)(2,1)}, bf16[2,128,8,...) while((s32[]{:T(128)}, bf16[2,128,8]{1,2,0:T(8,128)(2,1)S(1)}, ...), condition=%wide.region_4.5_spmd, body=%wide.region_1.4_spmd.sunk | while | flops 272768000 | bytes 13944989 | solution.py:59
  74.6 1.0 constant_dynamic-slice_fusion.3
  75.6 0.5 bitcast_reduce_fusion.2
  76.1 0.6 fusion.37
  76.7 0.8 fusion.39
  77.5 0.6 fusion.38
  78.3 1.0 constant_dynamic-slice_fusion.3
  79.3 0.5 bitcast_reduce_fusion.2
  79.8 0.6 fusion.37
  80.5 0.8 fusion.39
  81.2 0.6 fusion.38
  82.0 1.9 %copy_bitcast_fusion.2 = bf16[2,128,1024]{2,1,0:T(8,128)(2,1)} fusion(bf16[2,128,8,128]{3,1,2,0:T(8,128)(2,1)} %get-tuple-element.95), kind=kLoop, calls=%fused_computation.34 | loop fusion | bytes 1048576 | tf_op jit(solution)/shard_map/convert_element_type | solution.py:109
  84.0 10.9 %all_to_all.20 = bf16[2,128,8]{1,2,0:T(8,128)(2,1)S(1)} all-to-all(bf16[2,128,8]{1,2,0:T(8,128)(2,1)S(1)} %get-tuple-element.94), channel_id=1, replica_groups=mesh['parts'=2,'shard'=2,'blk'=8] {'shard'}, dimensions={0} | all-to-all | bytes 8192 | tf_op jit(solution)/shard_map/all_to_all | solution.py:115
  94.9 3.5 %all-to-all-start.3 = ((bf16[2,128,8]{1,2,0:T(8,128)(2,1)}), bf16[2,128,8]{1,2,0:T(8,128)(2,1)S(1)}, u32[]{:S(2)}, u32[]{:S(2)}) async-start(bf16[2,128,8]{1,2,0:T(8,128)(2,1)} %get-tuple-element.96), calls=%async_computation.3 | async-start | bytes 8192 | tf_op jit(solution)/shard_map/all_to_all | solution.py:122
  98.6 0.9 all-to-all-done.3
  99.5 3.8 %all-to-all-start.2 = ((bf16[2,128,1024]{2,1,0:T(8,128)(2,1)}), bf16[2,128,1024]{2,1,0:T(8,128)(2,1)S(1)}, u32[]{:S(2)}, u32[]{:S(2)}) async-start(bf16[2,128,1024]{2,1,0:T(8,128)(2,1)} %copy_bitcast_fusion.2), calls=%async_computation.2 | async-start | bytes 1048576 | tf_op jit(solution)/shard_map/all_to_all | solution.py:108
  103.4 0.6 gather_fusion
  104.1 0.6 gather_fusion.4
  104.9 0.7 gather_fusion.1
  105.6 0.6 gather_fusion.5
  106.9 1.6 %gather_fusion.2 = f32[128,1024]{1,0:T(8,128)} fusion(f32[128,1024]{1,0:T(8,128)S(1)} %get-tuple-element.141, s32[1024]{0:T(1024)S(1)} %pad_clamp_fusion.1), kind=kCustom, calls=%fused_computation.1.clone | custom fusion | bytes 1049088 | tf_op jit(solution)/shard_map/jit(_take)/gather | solution.py:137
  108.5 1.1 %select_bitcast_fusion.1 = f32[16,8,8,128]{3,1,2,0:T(8,128)S(1)} fusion(f32[128,1024]{1,0:T(8,128)} %gather_fusion.2, pred[128]{0:T(512)(128)(4,1)S(1)} %get-tuple-element.156), kind=kLoop, calls=%fused_computation.38 | loop fusion | flops 131072 | bytes 1048704
  109.7 0.9 copy.67
  110.6 0.8 gather_fusion.3
  111.6 0.8 copy-done.1
  112.4 0.3 fusion.15
  112.7 0.2 divide_convert_fusion
  113.0 0.8 copy.76
  (58 shorter events, 2.0 us)
Async XLA Ops:
  0.0 21.7 %copy-start = (bf16[1024,1024]{1,0:T(8,128)(2,1)S(1)}, bf16[1024,1024]{1,0:T(8,128)(2,1)}, u32[]{:S(2)}) copy-start(bf16[1024,1024]{1,0:T(8,128)(2,1)} %param.11) | copy-start | bytes 6291460
  1.2 11.2 %collective-permute-start = (bf16[64,1024]{0,1:T(8,128)(2,1)S(1)}, bf16[64,1024]{0,1:T(8,128)(2,1)S(1)}, u32[]{:S(2)}, u32[]{:S(2)}) collective-permute-start(bf16[64,1024]{0,1:T(8,128)(2,1)S(1)} %copy.50), channel_id=1, source_target_pairs={{0,1},{1,2},{2,3},{3,4},{4,5},{5,6},{6,7},{7,0},{8,9},{9,10},{10,1... | collective-permute-start | bytes 393224 | tf_op jit(solution)/shard_map/ppermute | solution.py:100
  12.4 9.3 %collective-permute-start.1 = (bf16[64,1024]{0,1:T(8,128)(2,1)S(1)}, bf16[64,1024]{0,1:T(8,128)(2,1)S(1)}, u32[]{:S(2)}, u32[]{:S(2)}) collective-permute-start(bf16[64,1024]{0,1:T(8,128)(2,1)S(1)} %collective-permute-done), channel_id=1, source_target_pairs={{0,1},{1,2},{2,3},{3,4},{4,5},{5,6},{6,7},{7,0},{8,9},{9,10},{10,1... | collective-permute-start | bytes 393224 | tf_op jit(solution)/shard_map/ppermute | solution.py:100
  21.7 8.5 %collective-permute-start.2 = (bf16[64,1024]{0,1:T(8,128)(2,1)S(1)}, bf16[64,1024]{0,1:T(8,128)(2,1)}, u32[]{:S(2)}, u32[]{:S(2)}) collective-permute-start(bf16[64,1024]{0,1:T(8,128)(2,1)S(1)} %collective-permute-done.1), channel_id=1, source_target_pairs={{0,1},{1,2},{2,3},{3,4},{4,5},{5,6},{6,7},{7,0},{8,9},{9,10},{10,1... | collective-permute-start | bytes 393224 | tf_op jit(solution)/shard_map/ppermute | solution.py:100
  24.1 31.7 %all-to-all-start = ((bf16[2,128,1024]{2,1,0:T(8,128)(2,1)}), bf16[2,128,1024]{2,1,0:T(8,128)(2,1)S(1)}, u32[]{:S(2)}, u32[]{:S(2)}) async-start(bf16[2,128,1024]{2,1,0:T(8,128)(2,1)} %convolution_convert_fusion), calls=%async_computation | async-start | bytes 1048576 | tf_op jit(solution)/shard_map/all_to_all | solution.py:95
  30.1 8.1 %collective-permute-start.3 = (bf16[64,1024]{0,1:T(8,128)(2,1)}, bf16[64,1024]{0,1:T(8,128)(2,1)S(1)}, u32[]{:S(2)}, u32[]{:S(2)}) collective-permute-start(bf16[64,1024]{0,1:T(8,128)(2,1)} %collective-permute-done.2), channel_id=1, source_target_pairs={{0,1},{1,2},{2,3},{3,4},{4,5},{5,6},{6,7},{7,0},{8,9},{9,10},{10,1... | collective-permute-start | bytes 393224 | tf_op jit(solution)/shard_map/ppermute | solution.py:100
  38.2 0.7 copy-start.2
  39.0 7.9 %collective-permute-start.4 = (bf16[64,1024]{0,1:T(8,128)(2,1)S(1)}, bf16[64,1024]{0,1:T(8,128)(2,1)S(1)}, u32[]{:S(2)}, u32[]{:S(2)}) collective-permute-start(bf16[64,1024]{0,1:T(8,128)(2,1)S(1)} %collective-permute-done.3), channel_id=1, source_target_pairs={{0,1},{1,2},{2,3},{3,4},{4,5},{5,6},{6,7},{7,0},{8,9},{9,10},{10,1... | collective-permute-start | bytes 393224 | tf_op jit(solution)/shard_map/ppermute | solution.py:100
  46.9 0.7 copy-start.3
  47.6 8.0 %collective-permute-start.5 = (bf16[64,1024]{0,1:T(8,128)(2,1)S(1)}, bf16[64,1024]{0,1:T(8,128)(2,1)}, u32[]{:S(2)}, u32[]{:S(2)}) collective-permute-start(bf16[64,1024]{0,1:T(8,128)(2,1)S(1)} %collective-permute-done.4), channel_id=1, source_target_pairs={{0,1},{1,2},{2,3},{3,4},{4,5},{5,6},{6,7},{7,0},{8,9},{9,10},{10,1... | collective-permute-start | bytes 393224 | tf_op jit(solution)/shard_map/ppermute | solution.py:100
  55.6 8.6 %collective-permute-start.6 = (bf16[64,1024]{0,1:T(8,128)(2,1)}, bf16[64,1024]{0,1:T(8,128)(2,1)}, u32[]{:S(2)}, u32[]{:S(2)}) collective-permute-start(bf16[64,1024]{0,1:T(8,128)(2,1)} %collective-permute-done.5), channel_id=1, source_target_pairs={{0,1},{1,2},{2,3},{3,4},{4,5},{5,6},{6,7},{7,0},{8,9},{9,10},{10,1... | collective-permute-start | bytes 393224 | tf_op jit(solution)/shard_map/ppermute | solution.py:100
  75.6 1.1 %copy-start.4 = (bf16[2,128,8,128]{3,1,2,0:T(8,128)(2,1)S(1)}, bf16[2,128,8,128]{3,1,2,0:T(8,128)(2,1)}, u32[]{:S(2)}) copy-start(bf16[2,128,8,128]{3,1,2,0:T(8,128)(2,1)} %get-tuple-element.212) | copy-start | bytes 1572868 | tf_op jit(solution)/shard_map/while/body/eval_jaxpr/while
  77.5 0.8 copy-start.5
  79.3 1.1 %copy-start.4 = (bf16[2,128,8,128]{3,1,2,0:T(8,128)(2,1)S(1)}, bf16[2,128,8,128]{3,1,2,0:T(8,128)(2,1)}, u32[]{:S(2)}) copy-start(bf16[2,128,8,128]{3,1,2,0:T(8,128)(2,1)} %get-tuple-element.212) | copy-start | bytes 1572868 | tf_op jit(solution)/shard_map/while/body/eval_jaxpr/while
  81.2 0.8 copy-start.5
  94.9 4.5 %all-to-all-start.3 = ((bf16[2,128,8]{1,2,0:T(8,128)(2,1)}), bf16[2,128,8]{1,2,0:T(8,128)(2,1)S(1)}, u32[]{:S(2)}, u32[]{:S(2)}) async-start(bf16[2,128,8]{1,2,0:T(8,128)(2,1)} %get-tuple-element.96), calls=%async_computation.3 | async-start | bytes 8192 | tf_op jit(solution)/shard_map/all_to_all | solution.py:122
  99.5 7.3 %all-to-all-start.2 = ((bf16[2,128,1024]{2,1,0:T(8,128)(2,1)}), bf16[2,128,1024]{2,1,0:T(8,128)(2,1)S(1)}, u32[]{:S(2)}, u32[]{:S(2)}) async-start(bf16[2,128,1024]{2,1,0:T(8,128)(2,1)} %copy_bitcast_fusion.2), calls=%async_computation.2 | async-start | bytes 1048576 | tf_op jit(solution)/shard_map/all_to_all | solution.py:108
  111.4 1.0 copy-start.1
